TPU v7x, 256 devices: a whole 4x4x8 slice. The times are simulated.
256 devices in a mesh: leaf: 64 (over y_lo, x, z), blk: 4 (over y_hi, core).
Axes of the slice: x: 4, y: 4 (y_hi: 2, y_lo: 2; y = y_hi * 2 + y_lo), z: 8, core: 2. Of those that a mesh axis runs over, the one named last changes fastest.
Arguments:
- root_front_inverse: float32 [2048, 2048], P('leaf', 'blk'), as said below
- child_front_inverse: float32 [65536, 1024], P('leaf', 'blk'), as said below
- child_coupling_block: float32 [32768, 1024], P('leaf', 'blk'), may hold values from -0.375 to 0.375
- coupled_root_blocks: int32 [64, 4], P('leaf'), may hold values from 0 to 15, as said below
- jacobian_child_index: int32 [6, 131072], P(None, ('leaf', 'blk')), may hold values from 0 to 1023
- jacobian_child_value: float32 [6, 131072], P(None, ('leaf', 'blk')), may hold values from -6 to 6
- jacobian_root_index: int32 [2, 131072], P(None, ('leaf', 'blk')), may hold values from 0 to 511
- jacobian_root_value: float32 [2, 131072], P(None, ('leaf', 'blk')), may hold values from -6 to 6
- resid: float32 [131072], P(('leaf', 'blk')), may hold values from -6 to 6
- noise_variance: float32 [131072], P(('leaf', 'blk')), may hold values from 0.05 to 1
- device_active_count: int32 [256], P(('leaf', 'blk')), may hold values from 1 to 512, 65536 in all
Outputs:
- normalized: float32 [131072], P(('leaf', 'blk'))
Inputs may be any that keep to these rules, and one draw needn't show every extreme that they name: root_front_inverse is lower triangular with a positive diagonal. Each 1024 x 1024 block of child_front_inverse is lower triangular with a positive diagonal. `coupled_root_blocks`: each row names 4 different root blocks.
All inputs are finite; a program needn't handle non-finite values. No bound on the sum of `device_active_count` on one device may be relied on, other than what follows from the above.
Results may differ from a plain program's by a relative error of at most 0.0003.
Values sent between devices are 32-bit elements; how exact they have to be, the bound alone decides.
A program may use at most 64 MiB of HBM per device.

v0:
```python
import jax
import jax.numpy as jnp
from jax import lax
from jax.sharding import PartitionSpec as P

B = 128


def per_device(
    root_front_inverse,
    child_front_inverse,
    child_coupling_block,
    coupled_root_blocks,
    jacobian_child_index,
    jacobian_child_value,
    jacobian_root_index,
    jacobian_root_value,
    resid,
    noise_variance,
    device_active_count,
):
    high = lax.Precision.HIGHEST
    cols_loc = root_front_inverse.shape[1]
    count_rows = coupled_root_blocks.shape[1] * B
    offsets = jnp.arange(count_rows, dtype=jnp.int32)
    rows_need = coupled_root_blocks[0][offsets // B] * B + offsets % B
    full_rows = lax.all_gather(root_front_inverse, "blk", axis=1, tiled=True)
    piece = full_rows
    mine = lax.psum_scatter(
        jnp.dot(piece.T, root_front_inverse, precision=high, preferred_element_type=jnp.float32),
        "leaf",
        scatter_dimension=0,
        tiled=True,
    )
    piece = lax.all_gather(mine, "leaf", axis=0, tiled=True)
    height = piece.shape[0]
    inside = (rows_need >= 0) & (rows_need < height)
    taken = jnp.take(piece, jnp.clip(rows_need, 0, height - 1), axis=0)
    slab = jnp.where(inside[:, None], taken, jnp.zeros((count_rows, cols_loc), jnp.float32))
    local_cols = rows_need - lax.axis_index("blk") * cols_loc
    inside_cols = (local_cols >= 0) & (local_cols < cols_loc)
    picked = jnp.take(slab, jnp.clip(local_cols, 0, cols_loc - 1), axis=1)
    ancestor = lax.psum(jnp.where(inside_cols[None, :], picked, jnp.float32(0.0)), "blk")
    inv_full, off_full = (
        lax.all_gather(child_front_inverse, "blk", axis=1, tiled=True),
        lax.all_gather(child_coupling_block, "blk", axis=1, tiled=True),
    )
    slot_positions = resid.shape[0]
    inv_cols = jnp.zeros((inv_full.shape[0], slot_positions), jnp.float32)
    for k in range(jacobian_child_index.shape[0]):
        inv_cols = (
            inv_cols
            + jnp.take(inv_full, jacobian_child_index[k], axis=1) * jacobian_child_value[k][None, :]
        )
    root_part = jnp.zeros((count_rows, slot_positions), jnp.float32)
    for k in range(jacobian_root_index.shape[0]):
        root_part = root_part + jnp.where(
            offsets[:, None] == jacobian_root_index[k][None, :],
            jacobian_root_value[k][None, :],
            jnp.float32(0.0),
        )
    gap = (
        jnp.dot(off_full, inv_cols, precision=high, preferred_element_type=jnp.float32) - root_part
    )
    weighted = jnp.dot(ancestor, gap, precision=high, preferred_element_type=jnp.float32)
    omega = noise_variance + jnp.sum(inv_cols * inv_cols, axis=0) + jnp.sum(gap * weighted, axis=0)
    active_slot_mask = jnp.arange(slot_positions, dtype=jnp.int32) < device_active_count[0]
    return jnp.where(active_slot_mask, resid / jnp.sqrt(omega), jnp.float32(0.0))


def solution(mesh):
    placed = (
        P("leaf", "blk"),
        P("leaf", "blk"),
        P("leaf", "blk"),
        P("leaf", None),
        P(None, ("leaf", "blk")),
        P(None, ("leaf", "blk")),
        P(None, ("leaf", "blk")),
        P(None, ("leaf", "blk")),
        P(("leaf", "blk")),
        P(("leaf", "blk")),
        P(("leaf", "blk")),
    )
    return jax.shard_map(
        per_device, mesh=mesh, in_specs=placed, out_specs=P(("leaf", "blk")), check_vma=False
    )
```

profile of v0, /device:TPU:25, one launch (start us, length us, event | category | flops | bytes accessed | tf_op | source)
XLA Modules:
  0.0 735.7 jit_solution(5271191208633313996)
XLA Ops:
  7.4 8.0 %all_gather.14 = f32[32,2048]{1,0:T(8,128)S(1)} all-gather(f32[32,512]{1,0:T(8,128)} %param.13), channel_id=1, replica_groups=mesh['leaf'=64,'blk'=4] {'blk'}, dimensions={1}, use_global_device_ids=true | all-gather | bytes 327680 | tf_op jit(solution)/shard_map/all_gather | solution.py:27
  15.4 5.9 fusion.20
  21.4 1.1 copy-done
  22.5 1.3 copy.14
  23.9 273.0 %reduce-scatter.2.cloned.1.call-done = f32[32,512]{1,0:T(8,128)} async-done(((f32[2048,512]{1,0:T(8,128)}), f32[32,512]{1,0:T(8,128)}) %reduce-scatter.2.cloned.1.call-update) | async-done | bytes 65552 | tf_op jit(solution)/shard_map/reduce_scatter | solution.py:29
  298.6 2.5 fusion.9
  301.7 2.5 compare_select_fusion
  304.5 5.0 gather_fusion.4
  309.5 5.8 gather_fusion.5
  315.3 5.8 gather_fusion.6
  321.1 5.8 gather_fusion.7
  326.9 5.8 gather_fusion.2
  332.7 5.8 gather_fusion.3
  338.4 259.7 %all-gather.8.cloned.1.call-done = f32[2048,512]{1,0:T(8,128)} async-done(((f32[32,512]{1,0:T(8,128)}), f32[2048,512]{1,0:T(8,128)}) %all-gather.8.cloned.1.call-update) | async-done | bytes 4194320 | tf_op jit(solution)/shard_map/all_gather | solution.py:35
  598.1 4.2 gather_fusion
  602.3 1.2 select_select_fusion
  603.5 1.6 copy.15
  605.1 2.3 gather_fusion.1
  607.4 2.4 select_bitcast_fusion
  609.9 6.0 multiply_reduce_fusion
  615.9 55.7 %all-gather.6.cloned.1.call-done = f32[512,1024]{1,0:T(8,128)} async-done(((f32[512,256]{1,0:T(8,128)}), f32[512,1024]{1,0:T(8,128)}) %all-gather.6.cloned.1.call-update) | async-done | bytes 2097168 | tf_op jit(solution)/shard_map/all_gather | solution.py:46
  671.5 5.8 fusion.5
  677.3 47.0 %all-reduce.2.cloned.1.call-done = f32[512,512]{0,1:T(8,128)} async-done(((f32[512,512]{0,1:T(8,128)}), f32[512,512]{0,1:T(8,128)}) %all-reduce.2.cloned.1.call-update) | async-done | bytes 1048592 | tf_op jit(solution)/shard_map/psum | solution.py:43
  724.3 3.1 fusion.6
  (51 shorter events, 2.4 us)
Async XLA Ops:
  7.4 289.6 %reduce-scatter.2.cloned.1.call-start = ((), (), s32[]{:S(2)}) async-start(), calls=%async_computation.3 | async-start | bytes 4259840 | tf_op jit(solution)/shard_map/reduce_scatter | solution.py:29
  21.3 1.2 copy-start
  21.3 276.4 %copy-start.1 = (s32[6,512]{1,0:T(8,128)S(1)}, s32[6,512]{1,0:T(8,128)}, u32[]{:S(2)}) copy-start(s32[6,512]{1,0:T(8,128)} %param.17) | copy-start | bytes 36868
  21.3 276.6 %copy-start.3 = (s32[1,4]{1,0:T(1,128)S(1)}, s32[1,4]{1,0:T(1,128)}, u32[]{:S(2)}) copy-start(s32[1,4]{1,0:T(1,128)} %param.16) | copy-start | bytes 52
  21.3 283.0 %copy-start.4 = (s32[2,512]{1,0:T(2,128)S(1)}, s32[2,512]{1,0:T(2,128)}, u32[]{:S(2)}) copy-start(s32[2,512]{1,0:T(2,128)} %param.19) | copy-start | bytes 12292
  21.4 283.0 %copy-start.5 = (f32[2,512]{1,0:T(2,128)S(1)}, f32[2,512]{1,0:T(2,128)}, u32[]{:S(2)}) copy-start(f32[2,512]{1,0:T(2,128)} %param.20) | copy-start | bytes 12292
  21.4 283.1 %copy-start.2 = (f32[6,512]{1,0:T(8,128)S(1)}, f32[6,512]{1,0:T(8,128)}, u32[]{:S(2)}) copy-start(f32[6,512]{1,0:T(8,128)} %param.18) | copy-start | bytes 36868
  21.4 283.1 %all-gather.4.cloned.1.call-start = ((), (), s32[]{:S(2)}) async-start(), calls=%async_computation.1 | async-start | bytes 5242880 | tf_op jit(solution)/shard_map/all_gather | solution.py:45
  23.9 574.3 %all-gather.8.cloned.1.call-start = ((), (), s32[]{:S(2)}) async-start(), calls=%async_computation.4 | async-start | bytes 4259840 | tf_op jit(solution)/shard_map/all_gather | solution.py:35
  297.0 374.6 %all-gather.6.cloned.1.call-start = ((), (), s32[]{:S(2)}) async-start(), calls=%async_computation.2 | async-start | bytes 2621440 | tf_op jit(solution)/shard_map/all_gather | solution.py:46
  297.5 426.8 %all-reduce.2.cloned.1.call-start = ((), (), s32[]{:S(2)}) async-start(), calls=%async_computation.5 | async-start | bytes 2097152 | tf_op jit(solution)/shard_map/psum | solution.py:43
  677.3 50.1 %copy-start.6 = (f32[512]{0:T(512)S(1)}, f32[512]{0:T(512)}, u32[]{:S(2)}) copy-start(f32[512]{0:T(512)} %param.21) | copy-start | bytes 6148
  677.3 50.1 %copy-start.7 = (f32[512]{0:T(512)S(1)}, f32[512]{0:T(512)}, u32[]{:S(2)}) copy-start(f32[512]{0:T(512)} %param.22) | copy-start | bytes 6148
Sparse Core Ops, SparseCore 0:
  21.4 275.4 reduce-scatter.1
Sparse Core Ops, SparseCore 1:
  23.9 46.5 all-gather.3
  297.0 301.0 all-gather.7
  599.9 71.5 all-gather.5
  674.4 49.9 all-reduce.1
where the time goes:
time: 739 us; the launch traced here: 736 us
  waiting for transfers between devices  636 us (86%)
  local copies, waits for them, and re-layouts  45.2 us (6%)
  between operations  16.1 us (2%)
  other arithmetic  15.3 us (2%)
  matrix products  14.8 us (2%)
  blocking collectives  8 us (1%)
    reduce_scatter x1, waiting for transfers between devices, per_device(): lax.psum_scatter(jnp.dot(piece.T, root_front_inverse, precision=high, pre...  273 us
    all_gather x1, waiting for transfers between devices, per_device(): piece = lax.all_gather(mine, 'leaf', axis=0, tiled=True)  260 us
    all_gather x1, waiting for transfers between devices, per_device(): lax.all_gather(child_coupling_block, 'blk', axis=1, tiled=True)  55.7 us
    psum x1, waiting for transfers between devices, per_device(): lax.psum(jnp.where(inside_cols[None, :], picked, jnp.float32(0.0)), 'blk')  47 us
    gather x6, local copies, waits for them, and re-layouts, per_device(): jnp.take(inv_full, jacobian_child_index[k], axis=1)  34 us
  transfers between devices with their start and end apart: 5, of which 4 were waited for; matrix products, arithmetic and copies ran while one was open for 9% of the time, Pallas kernels for 0%

commit v1 on v0

v1 whole, which is shorter than its diff:
```python
import functools

import jax
import jax.numpy as jnp
from jax import lax
from jax.experimental import pallas as pl
from jax.experimental.pallas import tpu as pltpu
from jax.sharding import PartitionSpec as P

MESH = pl.DeviceIdType.MESH
HIGH = lax.Precision.HIGHEST
TILES = 18


def dot(a, b):
    return jnp.dot(a, b, precision=HIGH, preferred_element_type=jnp.float32)


def dot_t(a, b):
    return lax.dot_general(
        a, b, (((0,), (0,)), ((), ())), precision=HIGH, preferred_element_type=jnp.float32
    )


def kernel(
    l_ref, f_ref, c_ref, sel_ref, jci_ref, jcv_ref, jri_ref, jrv_ref, resid_ref, noise_ref, count_ref,
    out_ref,
    l_buf, z_own, z_oth, f_buf, c_buf, j_buf, v_buf, g_buf, s_buf, a_send, a_recv, a_sum, sel_buf, sel_sm,
    l_send, l_recv, z_send, z_recv, d_send, d_recv, sel_send, sel_recv,
    fc_send, fc_recv, cc_send, cc_recv, x_send, x_recv, as_send, as_recv,
):
    leaf = lax.axis_index("leaf")
    blk = lax.axis_index("blk")
    ylo, x, z = lax.div(leaf, 32), lax.rem(lax.div(leaf, 8), 4), lax.rem(leaf, 8)
    yhi, core = lax.div(blk, 2), lax.rem(blk, 2)

    def device(ylo_d, x_d, z_d, blk_d):
        return {"leaf": ylo_d * 32 + x_d * 8 + z_d, "blk": blk_d}

    def copy(src, dst, send, recv, to):
        return pltpu.make_async_remote_copy(
            src_ref=src, dst_ref=dst, send_sem=send, recv_sem=recv, device_id=to, device_id_type=MESH
        )

    mirror = 3 - x
    zr, zl = lax.rem(z + 1, 8), lax.rem(z + 7, 8)
    right, left = device(ylo, x, zr, blk), device(ylo, x, zl, blk)
    mate_blk = 2 * yhi + 1 - core
    mate = device(ylo, x, z, mate_blk)
    across_blk = 2 * (1 - yhi) + core
    across = device(ylo, x, z, across_blk)
    far_blk = 2 * (1 - yhi) + 1 - core

    barrier = pltpu.get_barrier_semaphore()
    partners = [right, left]
    for ylo_d in range(2):
        for blk_d in range(4):
            partners.append(device(ylo_d, mirror, z, blk_d))
    for d_ylo in range(2):
        for d_blk in range(4):
            if (d_ylo, d_blk) != (0, 0):
                partners.append(device(lax.rem(ylo + d_ylo, 2), x, z, lax.rem(blk + d_blk, 4)))
    even = lax.rem(x, 2)
    other_near = lax.rem(x + jnp.where(even == 0, 1, 3), 4)
    partners.append(device(ylo, lax.rem(x + 2, 4), z, blk))
    partners.append(device(ylo, other_near, z, blk))
    for p in partners:
        pl.semaphore_signal(barrier, inc=1, device_id=p, device_id_type=MESH)
    pl.semaphore_wait(barrier, len(partners))

    for core_d in range(2):
        for h in range(2):
            for u in range(2):
                for q in range(2):
                    l_buf[core_d, h, u, q] = l_ref[
                        16 * core_d + 8 * u : 16 * core_d + 8 * u + 8, 256 * h + 128 * q : 256 * h + 128 * q + 128
                    ]
    upper = ylo == 0
    x_to = jnp.where(upper, x, mirror)
    for h in range(2):
        tile = 2 * blk + h
        slot = jnp.where(upper, tile, 4 - x + tile)
        valid = jnp.where(upper, tile <= x, tile <= 4 + x)
        for ylo_d in range(2):
            for blk_d in range(4):
                core_d = blk_d % 2
                src = l_buf.at[core_d, h]
                self_ = upper & (ylo_d == ylo) & (blk_d == blk)
                dst = z_own.at[0, :, pl.ds(2 * slot, 2)]

                @pl.when(valid & jnp.logical_not(self_))
                def _():
                    copy(
                        src, dst, l_send.at[h, ylo_d, blk_d], l_recv.at[slot],
                        device(ylo_d, x_to, z, blk_d),
                    ).start()

                @pl.when(valid & self_)
                def _():
                    pltpu.make_async_copy(src, dst, l_recv.at[slot]).start()

    sel_copies = []
    for d in range(1, 4):
        cp = copy(
            sel_ref, sel_buf.at[4 - d], sel_send.at[d], sel_recv.at[4 - d],
            device(ylo, lax.rem(x + d, 4), z, blk),
        )
        cp.start()
        sel_copies.append(cp)
    own_sel = pltpu.make_async_copy(sel_ref, sel_buf.at[0], sel_recv.at[0])
    own_sel.start()

    def f_rows(r):
        return pl.ds(256 * r, 256)

    def f_copy(kind, r):
        if kind == 0:
            return copy(f_ref.at[f_rows(r)], f_buf.at[blk, f_rows(r)], fc_send.at[0, r], fc_recv.at[0, r], mate)
        if kind == 1:
            return copy(f_ref.at[f_rows(r)], f_buf.at[blk, f_rows(r)], fc_send.at[1, r], fc_recv.at[1, r], across)
        return copy(
            f_buf.at[across_blk, f_rows(r)], f_buf.at[across_blk, f_rows(r)], fc_send.at[2, r], fc_recv.at[2, r], mate
        )

    def c_copy(kind, r):
        if kind == 0:
            return copy(c_ref.at[f_rows(r)], c_buf.at[blk, f_rows(r)], cc_send.at[0, r], cc_recv.at[0, r], mate)
        if kind == 1:
            return copy(c_ref.at[f_rows(r)], c_buf.at[blk, f_rows(r)], cc_send.at[1, r], cc_recv.at[1, r], across)
        return copy(
            c_buf.at[across_blk, f_rows(r)], c_buf.at[across_blk, f_rows(r)], cc_send.at[2, r], cc_recv.at[2, r], mate
        )

    f_own = [pltpu.make_async_copy(f_ref.at[f_rows(r)], f_buf.at[blk, f_rows(r)], fc_recv.at[3, r]) for r in range(4)]
    c_own = [pltpu.make_async_copy(c_ref.at[f_rows(r)], c_buf.at[blk, f_rows(r)], cc_recv.at[3, r]) for r in range(2)]

    for kind in (1, 0):
        for r in range(4):

            @pl.when(r >= blk)
            def _():
                f_copy(kind, r).start()

        for r in range(2):
            c_copy(kind, r).start()
    for r in range(4):

        @pl.when(r >= blk)
        def _():
            f_own[r].start()

    for r in range(2):
        c_own[r].start()

    @pl.loop(0, 16)
    def _(i):
        rows = lax.broadcasted_iota(jnp.int32, (64, 512), 0) + i * 64
        acc = jnp.zeros((64, 512), jnp.float32)
        for k in range(6):
            acc = acc + jnp.where(rows == jci_ref[k : k + 1, :], jcv_ref[k : k + 1, :], 0.0)
        j_buf[pl.ds(pl.multiple_of(i * 64, 64), 64), :] = acc

    for slot in range(9):
        tile = z_own.at[0, :, pl.ds(2 * slot, 2)]
        pltpu.make_async_copy(tile, tile, l_recv.at[slot]).wait()

    def sub(ref, s, u):
        return ref.at[s, u]

    z_copies = []

    def ring(s, u, way):
        to = s + 1 if way == 0 else (s + 7) % 8
        cp = copy(sub(z_own, s, u), sub(z_own, to, u), z_send.at[way, s, u], z_recv.at[to, u], right if way == 0 else left)
        cp.start()
        z_copies.append(cp)

    def share(s, u):
        cp = copy(sub(z_own, s, u), sub(z_oth, s, u), d_send.at[s, u], d_recv.at[s, u], mate)
        cp.start()
        return cp

    shares = []

    def arrived(s, u):
        pltpu.make_async_copy(sub(z_own, s, u), sub(z_own, s, u), z_recv.at[s, u]).wait()

    for u in range(2):
        ring(0, u, 0)
        ring(0, u, 1)
    for u in range(2):
        shares.append(share(0, u))
    for s in range(1, 4):
        for u in range(2):
            arrived(s, u)
            if s < 3 or u == 0:
                ring(s, u, 0)
            shares.append(share(s, u))
            arrived(8 - s, u)
            if s < 3 or u == 1:
                ring(8 - s, u, 1)
            shares.append(share(8 - s, u))
    for u in range(2):
        arrived(4, u)
        shares.append(share(4, u))
    for cp in sel_copies:
        cp.wait()
    own_sel.wait()
    pltpu.sync_copy(sel_buf, sel_sm)
    for cp in shares:
        cp.wait()

    x_copies = []
    for d in (2, 1, 3, 0):
        for i in range(4):
            j = sel_sm[d, lax.rem(i + core, 4), 0]
            choice = sel_buf[d, pl.ds(lax.rem(i + core, 4), 1), :]
            hi0 = 2 * x + 1
            hi1 = 15 - 2 * x
            below = 2 * (x + 1) + jnp.minimum(j, hi1)
            at = pl.ds(i * 128, 128)
            for n, ref in enumerate((z_own, z_oth)):
                part = ref[:, :, j].reshape(128, 128)
                s_buf[pl.ds(256 * n, 128), at] = jnp.where(choice <= hi0, part, 0.0)
                part = ref[:, :, below].reshape(128, 128)
                s_buf[pl.ds(256 * n + 128, 128), at] = jnp.where(choice <= hi1, part, 0.0)
        first = dot_t(s_buf[:, 0:128], s_buf[:, 0:384])
        second = dot_t(s_buf[:, 256:384], s_buf[:, 256:512])
        a_send[d, :, 0:128] = first[:, 0:128]
        a_send[d, :, 128:384] = 2.0 * first[:, 128:384]
        a_send[d, :, 384:512] = second[:, 0:128]
        a_send[d, :, 512:640] = 2.0 * second[:, 128:256]
        if d:
            cp = copy(
                a_send.at[d], a_recv.at[4 - d], x_send.at[d], x_recv.at[4 - d],
                device(ylo, lax.rem(x + d, 4), z, blk),
            )
            cp.start()
            x_copies.append(cp)

    for r in range(4):

        @pl.when(r >= across_blk)
        def _():
            f_copy(1, r).wait_recv()
            f_copy(2, r).start()

    for r in range(2):
        c_copy(1, r).wait_recv()
        c_copy(2, r).start()
    for r in range(4):

        @pl.when(r >= blk)
        def _():
            f_own[r].wait()

        @pl.when(r >= mate_blk)
        def _():
            f_copy(0, r).wait_recv()

        @pl.when(r >= far_blk)
        def _():
            f_copy(2, r).wait_recv()

    square = jnp.zeros((1, 512), jnp.float32)
    for r in range(4):
        acc = dot(f_buf[0, 256 * r : 256 * r + 256, :], j_buf[0:256, :])
        for s in range(1, r + 1):
            acc = acc + dot(f_buf[s, 256 * r : 256 * r + 256, :], j_buf[256 * s : 256 * s + 256, :])
        v_buf[256 * r : 256 * r + 256, :] = acc
        square = square + jnp.sum(acc * acc, axis=0, keepdims=True)

    for r in range(2):
        c_own[r].wait()
        c_copy(0, r).wait_recv()
        c_copy(2, r).wait_recv()
    for q in range(4):
        rows = lax.broadcasted_iota(jnp.int32, (128, 512), 0) + q * 128
        root = jnp.zeros((128, 512), jnp.float32)
        for k in range(2):
            root = root + jnp.where(rows == jri_ref[k : k + 1, :], jrv_ref[k : k + 1, :], 0.0)
        acc = dot(c_buf[0, 128 * q : 128 * q + 128, :], v_buf[0:256, :])
        for s in range(1, 4):
            acc = acc + dot(c_buf[s, 128 * q : 128 * q + 128, :], v_buf[256 * s : 256 * s + 256, :])
        acc = acc - root
        g_buf[128 * q : 128 * q + 128, :] = acc
        if q == 0:
            g_buf[512:640, :] = acc

    for cp in x_copies:
        cp.wait_recv()
    a_sum[0] = a_send[0] + a_recv[1] + a_recv[2] + a_recv[3]
    a_share = copy(a_sum.at[0], a_sum.at[1], as_send, as_recv, mate)
    a_share.start()

    def quad(n, c):
        start = pl.multiple_of(c * 128, 128)
        w = dot(a_sum[n, :, 0:384], g_buf[pl.ds(start, 384), :])
        q = jnp.sum(w * g_buf[pl.ds(start, 128), :], axis=0, keepdims=True)
        start = pl.multiple_of(c * 128 + 256, 128)
        w = dot(a_sum[n, :, 384:640], g_buf[pl.ds(start, 256), :])
        return q + jnp.sum(w * g_buf[pl.ds(start, 128), :], axis=0, keepdims=True)

    omega = noise_ref[...] + square + quad(0, core)
    a_share.wait()
    omega = omega + quad(1, 1 - core)
    live = lax.broadcasted_iota(jnp.int32, (1, 512), 1) < count_ref[0]
    out_ref[...] = jnp.where(live, resid_ref[...] / jnp.sqrt(omega), 0.0)

    for h in range(2):
        tile = 2 * blk + h
        valid = jnp.where(upper, tile <= x, tile <= 4 + x)
        for ylo_d in range(2):
            for blk_d in range(4):
                self_ = upper & (ylo_d == ylo) & (blk_d == blk)
                src = l_buf.at[0, h]

                @pl.when(valid & jnp.logical_not(self_))
                def _():
                    pltpu.make_async_copy(src, src, l_send.at[h, ylo_d, blk_d]).wait()

    for cp in z_copies:
        cp.wait_send()
    for cp in x_copies:
        cp.wait_send()
    for r in range(4):

        @pl.when(r >= blk)
        def _():
            f_copy(0, r).wait_send()
            f_copy(1, r).wait_send()

        @pl.when(r >= across_blk)
        def _():
            f_copy(2, r).wait_send()

    for r in range(2):
        for kind in range(3):
            c_copy(kind, r).wait_send()


def per_device(root, front, coupling, blocks, jci, jcv, jri, jrv, resid, noise, count):
    vmem = pl.BlockSpec(memory_space=pltpu.VMEM)
    anyspace = pl.BlockSpec(memory_space=pl.ANY)
    dma = pltpu.SemaphoreType.DMA
    f32 = jnp.float32
    sel = jnp.broadcast_to(jnp.concatenate([blocks[0], blocks[0]])[:, None], (8, 128))
    out = pl.pallas_call(
        kernel,
        out_shape=jax.ShapeDtypeStruct((1, 512), f32),
        in_specs=[vmem] + [anyspace] * 2 + [vmem] * 7 + [pl.BlockSpec(memory_space=pltpu.SMEM)],
        out_specs=vmem,
        scratch_shapes=[
            pltpu.VMEM((2, 2, 2, 2, 8, 128), f32),
            pltpu.VMEM((8, 2, TILES, 8, 128), f32),
            pltpu.VMEM((8, 2, TILES, 8, 128), f32),
            pltpu.VMEM((4, 1024, 256), f32),
            pltpu.VMEM((4, 512, 256), f32),
            pltpu.VMEM((1024, 512), f32),
            pltpu.VMEM((1024, 512), f32),
            pltpu.VMEM((640, 512), f32),
            pltpu.VMEM((512, 512), f32),
            pltpu.VMEM((4, 128, 640), f32),
            pltpu.VMEM((4, 128, 640), f32),
            pltpu.VMEM((2, 128, 640), f32),
            pltpu.VMEM((4, 8, 128), jnp.int32),
            pltpu.SMEM((4, 8, 128), jnp.int32),
            dma((2, 2, 4)), dma((9,)), dma((2, 8, 2)), dma((8, 2)), dma((8, 2)), dma((8, 2)),
            dma((4,)), dma((4,)),
            dma((3, 4)), dma((4, 4)), dma((3, 2)), dma((4, 2)),
            dma((4,)), dma((4,)), dma, dma,
        ],
        compiler_params=pltpu.CompilerParams(
            collective_id=0, has_side_effects=True, vmem_limit_bytes=48 << 20
        ),
        name="selected_inverse",
    )(
        root, front, coupling, sel, jci, jcv, jri, jrv,
        resid.reshape(1, -1), noise.reshape(1, -1), count,
    )
    return out.reshape(-1)


def solution(mesh):
    placed = (
        P("leaf", "blk"),
        P("leaf", "blk"),
        P("leaf", "blk"),
        P("leaf", None),
        P(None, ("leaf", "blk")),
        P(None, ("leaf", "blk")),
        P(None, ("leaf", "blk")),
        P(None, ("leaf", "blk")),
        P(("leaf", "blk")),
        P(("leaf", "blk")),
        P(("leaf", "blk")),
    )
    return jax.shard_map(
        per_device, mesh=mesh, in_specs=placed, out_specs=P(("leaf", "blk")), check_vma=False
    )
```

time: 739 us -> 64.4 us (0.09)
  waiting for transfers between devices: 636 us -> 0 us
  Pallas kernels: 0 us -> 57.2 us
  local copies, waits for them, and re-layouts: 45.2 us -> 5.74 us
  between operations: 16.1 us -> 0.72 us
  other arithmetic: 15.3 us -> 0.08 us
  matrix products: 14.8 us -> 0 us
  blocking collectives: 8 us -> 0 us
    all_gather x3 -> x0, waiting for transfers between devices: 315 us -> none  [the longest x1 260 us: per_device(): piece = lax.all_gather(mine, 'leaf', axis=0, tiled=True)]
    reduce_scatter x1 -> x0, waiting for transfers between devices: 273 us -> none  [per_device(): lax.psum_scatter(jnp.dot(piece.T, root_front_inverse, precision=high, pre...]
    pallas_call x0 -> x1, Pallas kernels: none -> 57.2 us  [per_device(): pl.pallas_call(kernel, out_shape=jax.ShapeDtypeStruct((1, 512), f32), in_...]
    psum x1 -> x0, waiting for transfers between devices: 47 us -> none  [per_device(): lax.psum(jnp.where(inside_cols[None, :], picked, jnp.float32(0.0)), 'blk')]
    gather x9 -> x0, local copies, waits for them, and re-layouts: 41.2 us -> none  [the longest x6 34 us: per_device(): jnp.take(inv_full, jacobian_child_index[k], axis=1)]
    dot_general x3 -> x0, matrix products: 14.8 us -> none  [the longest x1 5.92 us: per_device(): jnp.dot(piece.T, root_front_inverse, precision=high, preferred_element_ty...]
    all_gather x1 -> x0, blocking collectives: 8 us -> none  [per_device(): full_rows = lax.all_gather(root_front_inverse, 'blk', axis=1, tiled=True)]
  transfers between devices with their start and end apart: 5 -> 0, of which waited for: 4 -> 0; matrix products, arithmetic and copies ran while one was open for 9% -> 0% of each run, Pallas kernels for 0% -> 0%
where the time goes in v1:
time: 64.4 us; the launch traced here: 63.8 us
  Pallas kernels  57.2 us (89%)
  local copies, waits for them, and re-layouts  5.74 us (9%)
  between operations  0.72 us (1%)
    pallas_call x1, Pallas kernels, per_device(): pl.pallas_call(kernel, out_shape=jax.ShapeDtypeStruct((1, 512), f32), in_...  57.2 us
    unnamed x21, local copies, waits for them, and re-layouts  5.67 us

profile of v1, /device:TPU:25, one launch (start us, length us, event | category | flops | bytes accessed | tf_op | source)
XLA Modules:
  0.0 63.8 jit_solution(3865412282817382380)
XLA Ops:
  0.0 0.0 copy-start.9
  0.7 0.0 copy-start.8
  0.7 0.0 copy-start.7
  0.7 0.0 copy-start.5
  0.7 0.0 copy-start.6
  0.7 0.0 copy-done.9
  0.7 0.1 pad_add_fusion
  0.8 0.1 broadcast_in_dim.2.sel_ref
  0.9 0.5 copy-done.8
  1.4 0.0 copy-done.7
  1.4 0.0 copy-done.5
  1.4 0.0 copy-done.6
  1.4 0.0 copy-start
  1.4 1.2 %copy-done = f32[1024,256]{1,0:T(8,128)S(1)} copy-done((f32[1024,256]{1,0:T(8,128)S(1)}, f32[1024,256]{1,0:T(8,128)}, u32[]{:S(2)}) %copy-start) | copy-done | bytes 1048600
  2.6 0.0 copy-start.1
  2.6 1.0 %copy-done.1 = f32[512,256]{1,0:T(8,128)S(1)} copy-done((f32[512,256]{1,0:T(8,128)S(1)}, f32[512,256]{1,0:T(8,128)}, u32[]{:S(2)}) %copy-start.1) | copy-done | bytes 524312
  3.7 0.0 copy-start.2
  3.7 0.8 %copy-done.2 = f32[32,512]{1,0:T(8,128)S(1)} copy-done((f32[32,512]{1,0:T(8,128)S(1)}, f32[32,512]{1,0:T(8,128)}, u32[]{:S(2)}) %copy-start.2) | copy-done | bytes 65560
  4.5 0.0 copy-start.3
  4.5 0.7 %copy-done.3 = s32[6,512]{1,0:T(8,128)S(1)} copy-done((s32[6,512]{1,0:T(8,128)S(1)}, s32[6,512]{1,0:T(8,128)}, u32[]{:S(2)}) %copy-start.3) | copy-done | bytes 12312
  5.2 0.0 copy-start.4
  5.2 0.7 %copy-done.4 = f32[6,512]{1,0:T(8,128)S(1)} copy-done((f32[6,512]{1,0:T(8,128)S(1)}, f32[6,512]{1,0:T(8,128)}, u32[]{:S(2)}) %copy-start.4) | copy-done | bytes 12312
  5.9 57.2 %selected_inverse.1 = f32[1,512]{1,0:T(1,128)S(1)} custom-call(f32[32,512]{1,0:T(8,128)S(1)} %copy-done.2, f32[1024,256]{1,0:T(8,128)S(1)} %copy-done, f32[512,256]{1,0:T(8,128)S(1)} %copy-done.1, s32[8,128]{1,0:T(8,128)S(1)} %broadcast_in_dim.2.sel_ref, s32[6,512]{1,0:T(8,128)S(1)} %copy-done.3, f32[6,512]{1,0:T(8,128)S(1)} %copy-done.4, ...), custom_call_target="tpu_custom_call" | custom-call | tf_op jit(solution)/shard_map/selected_inverse/pallas_call | solution.py:348
  63.2 0.6 copy.14
Async XLA Ops:
  0.0 0.7 %copy-start.9 = (s32[1,4]{1,0:T(1,128)S(1)}, s32[1,4]{1,0:T(1,128)}, u32[]{:S(2)}) copy-start(s32[1,4]{1,0:T(1,128)} %param.14) | copy-start | bytes 52
  0.7 0.7 %copy-start.8 = (f32[512]{0:T(512)S(1)}, f32[512]{0:T(512)}, u32[]{:S(2)}) copy-start(f32[512]{0:T(512)} %param.20) | copy-start | bytes 6148
  0.7 0.7 %copy-start.7 = (f32[512]{0:T(512)S(1)}, f32[512]{0:T(512)}, u32[]{:S(2)}) copy-start(f32[512]{0:T(512)} %param.19) | copy-start | bytes 6148
  0.7 0.7 %copy-start.5 = (s32[2,512]{1,0:T(2,128)S(1)}, s32[2,512]{1,0:T(2,128)}, u32[]{:S(2)}) copy-start(s32[2,512]{1,0:T(2,128)} %jri_ref.1) | copy-start | bytes 12292
  0.7 0.7 %copy-start.6 = (f32[2,512]{1,0:T(2,128)S(1)}, f32[2,512]{1,0:T(2,128)}, u32[]{:S(2)}) copy-start(f32[2,512]{1,0:T(2,128)} %jrv_ref.1) | copy-start | bytes 12292
  1.4 1.2 %copy-start = (f32[1024,256]{1,0:T(8,128)S(1)}, f32[1024,256]{1,0:T(8,128)}, u32[]{:S(2)}) copy-start(f32[1024,256]{1,0:T(8,128)} %f_ref.1) | copy-start | bytes 3145732
  2.6 1.0 %copy-start.1 = (f32[512,256]{1,0:T(8,128)S(1)}, f32[512,256]{1,0:T(8,128)}, u32[]{:S(2)}) copy-start(f32[512,256]{1,0:T(8,128)} %c_ref.1) | copy-start | bytes 1572868
  3.7 0.8 %copy-start.2 = (f32[32,512]{1,0:T(8,128)S(1)}, f32[32,512]{1,0:T(8,128)}, u32[]{:S(2)}) copy-start(f32[32,512]{1,0:T(8,128)} %l_ref.1) | copy-start | bytes 196612
  4.5 0.7 %copy-start.3 = (s32[6,512]{1,0:T(8,128)S(1)}, s32[6,512]{1,0:T(8,128)}, u32[]{:S(2)}) copy-start(s32[6,512]{1,0:T(8,128)} %jci_ref.1) | copy-start | bytes 36868
  5.2 0.7 %copy-start.4 = (f32[6,512]{1,0:T(8,128)S(1)}, f32[6,512]{1,0:T(8,128)}, u32[]{:S(2)}) copy-start(f32[6,512]{1,0:T(8,128)} %jcv_ref.1) | copy-start | bytes 36868

commit v2 on v1

v2 whole, which is shorter than its diff:
```python
import functools

import jax
import jax.numpy as jnp
from jax import lax
from jax.experimental import pallas as pl
from jax.experimental.pallas import tpu as pltpu
from jax.sharding import PartitionSpec as P

MESH = pl.DeviceIdType.MESH
TILES = 18


def split(a):
    high = a.astype(jnp.bfloat16)
    return high, (a - high.astype(jnp.float32)).astype(jnp.bfloat16)


def dot(a, b, axis=1):
    def one(p, q):
        return lax.dot_general(p, q, (((axis,), (0,)), ((), ())), preferred_element_type=jnp.float32)

    return one(a[0], b[0]) + (one(a[0], b[1]) + one(a[1], b[0]))


def kernel(
    l_hbm, f_ref, c_ref, sel_hbm, jci_hbm, jcv_hbm, jri_hbm, jrv_hbm, resid_hbm, noise_hbm, count_hbm,
    out_ref,
    l_ref, sel_ref, jci_ref, jcv_ref, jri_ref, jrv_ref, resid_ref, noise_ref, sel_own, count_ref, in_sem,
    l_buf, z_own, z_oth, f_buf, c_buf, j_high, j_low, v_high, v_low, g_buf, g_high, g_low, s_high, s_low,
    a_send, a_pass, a_recv, a_sum, sel_buf, sel_sm,
    l_send, l_recv, z_send, z_recv, d_send, d_recv, sel_send, sel_recv,
    fc_send, fc_recv, cc_send, cc_recv, x_send, x_recv, as_send, as_recv,
):
    leaf = lax.axis_index("leaf")
    blk = lax.axis_index("blk")
    ylo, x, z = lax.div(leaf, 32), lax.rem(lax.div(leaf, 8), 4), lax.rem(leaf, 8)
    yhi, core = lax.div(blk, 2), lax.rem(blk, 2)

    def device(ylo_d, x_d, z_d, blk_d):
        return {"leaf": ylo_d * 32 + x_d * 8 + z_d, "blk": blk_d}

    def copy(src, dst, send, recv, to):
        return pltpu.make_async_remote_copy(
            src_ref=src, dst_ref=dst, send_sem=send, recv_sem=recv, device_id=to, device_id_type=MESH
        )

    zr, zl = lax.rem(z + 1, 8), lax.rem(z + 7, 8)
    right, left = device(ylo, x, zr, blk), device(ylo, x, zl, blk)
    mate_blk = 2 * yhi + 1 - core
    mate = device(ylo, x, z, mate_blk)
    across_blk = 2 * (1 - yhi) + core
    across = device(ylo, x, z, across_blk)
    far_blk = 2 * (1 - yhi) + 1 - core

    loads = [
        pltpu.make_async_copy(src, dst, in_sem.at[n])
        for n, (src, dst) in enumerate(
            [
                (l_hbm, l_ref), (sel_hbm, sel_own), (jci_hbm, jci_ref), (jcv_hbm, jcv_ref), (jri_hbm, jri_ref),
                (jrv_hbm, jrv_ref), (resid_hbm, resid_ref), (noise_hbm, noise_ref), (count_hbm, count_ref),
            ]
        )
    ]
    for cp in loads:
        cp.start()

    barrier = pltpu.get_barrier_semaphore()
    mirror = 3 - x
    near = lax.rem(x + jnp.where(lax.rem(x, 2) == 0, 1, 3), 4)
    partners = [right, left, device(ylo, lax.rem(x + 2, 4), z, blk), device(ylo, near, z, blk)]
    for ylo_d in range(2):
        for blk_d in range(4):
            partners.append(device(ylo_d, mirror, z, blk_d))
    for d_ylo in range(2):
        for d_blk in range(4):
            if (d_ylo, d_blk) != (0, 0):
                partners.append(device(lax.rem(ylo + d_ylo, 2), x, z, lax.rem(blk + d_blk, 4)))
    for p in partners:
        pl.semaphore_signal(barrier, inc=1, device_id=p, device_id_type=MESH)
    loads[0].wait()
    loads[1].wait()
    row = lax.broadcasted_iota(jnp.int32, (8, 128), 0)
    choices = jnp.zeros((8, 128), jnp.int32)
    for i in range(4):
        choices = jnp.where(row == i, sel_own[0, i], choices)
    sel_ref[...] = choices
    for h in range(2):
        for core_d in range(2):
            for u in range(2):
                for q in range(2):
                    r, c = 16 * core_d + 8 * u, 256 * h + 128 * q
                    l_buf[h, core_d, u, q] = l_ref[r : r + 8, c : c + 128]
    pl.semaphore_wait(barrier, len(partners))

    upper = ylo == 0
    spread = [(h, ylo_d, blk_d) for h in range(2) for ylo_d in range(2) for blk_d in range(4)]
    x_to = jnp.where(upper, x, mirror)

    def spread_copy(h, ylo_d, blk_d):
        slot = jnp.where(upper, 0, 4 - x) + 2 * blk + h
        return (
            l_buf.at[h, blk_d % 2], z_own.at[0, :, pl.ds(2 * slot, 2)],
            l_send.at[h, ylo_d, blk_d], l_recv.at[slot], device(ylo_d, x_to, z, blk_d),
        )

    def spread_valid(h, ylo_d, blk_d):
        valid = 2 * blk + h <= jnp.where(upper, x, 4 + x)
        mine = upper & (ylo_d == ylo) & (blk_d == blk)
        return valid & jnp.logical_not(mine), valid & mine

    for key in spread:
        away, here = spread_valid(*key)

        @pl.when(away)
        def _():
            copy(*spread_copy(*key)).start()

        @pl.when(here)
        def _():
            src, dst, _, sem, _ = spread_copy(*key)
            pltpu.make_async_copy(src, dst, sem).start()

    sel_copies = []
    for d in range(1, 4):
        cp = copy(
            sel_ref, sel_buf.at[4 - d], sel_send.at[d], sel_recv.at[4 - d],
            device(ylo, lax.rem(x + d, 4), z, blk),
        )
        cp.start()
        sel_copies.append(cp)
    own_sel = pltpu.make_async_copy(sel_ref, sel_buf.at[0], sel_recv.at[0])
    own_sel.start()

    def f_rows(r):
        return pl.ds(256 * r, 256)

    def f_copy(kind, r):
        if kind == 0:
            return copy(f_ref.at[f_rows(r)], f_buf.at[blk, f_rows(r)], fc_send.at[0, r], fc_recv.at[0, r], mate)
        if kind == 1:
            return copy(f_ref.at[f_rows(r)], f_buf.at[blk, f_rows(r)], fc_send.at[1, r], fc_recv.at[1, r], across)
        return copy(
            f_buf.at[across_blk, f_rows(r)], f_buf.at[across_blk, f_rows(r)], fc_send.at[2, r], fc_recv.at[2, r], mate
        )

    def c_copy(kind, r):
        if kind == 0:
            return copy(c_ref.at[f_rows(r)], c_buf.at[blk, f_rows(r)], cc_send.at[0, r], cc_recv.at[0, r], mate)
        if kind == 1:
            return copy(c_ref.at[f_rows(r)], c_buf.at[blk, f_rows(r)], cc_send.at[1, r], cc_recv.at[1, r], across)
        return copy(
            c_buf.at[across_blk, f_rows(r)], c_buf.at[across_blk, f_rows(r)], cc_send.at[2, r], cc_recv.at[2, r], mate
        )

    f_own = [pltpu.make_async_copy(f_ref.at[f_rows(r)], f_buf.at[blk, f_rows(r)], fc_recv.at[3, r]) for r in range(4)]
    c_own = [pltpu.make_async_copy(c_ref.at[f_rows(r)], c_buf.at[blk, f_rows(r)], cc_recv.at[3, r]) for r in range(2)]

    for kind in (1, 0):
        for r in range(4):

            @pl.when(r >= blk)
            def _():
                f_copy(kind, r).start()

        for r in range(2):
            c_copy(kind, r).start()
    for r in range(4):

        @pl.when(r >= blk)
        def _():
            f_own[r].start()

    for r in range(2):
        c_own[r].start()

    for cp in loads[2:]:
        cp.wait()

    @pl.loop(0, 16)
    def _(i):
        rows = lax.broadcasted_iota(jnp.int32, (64, 512), 0) + i * 64
        acc = jnp.zeros((64, 512), jnp.float32)
        for k in range(6):
            acc = acc + jnp.where(rows == jci_ref[k : k + 1, :], jcv_ref[k : k + 1, :], 0.0)
        at = pl.ds(pl.multiple_of(i * 64, 64), 64)
        j_high[at, :], j_low[at, :] = split(acc)

    for slot in range(9):
        tile = z_own.at[0, :, pl.ds(2 * slot, 2)]
        pltpu.make_async_copy(tile, tile, l_recv.at[slot]).wait()

    def sub(ref, s, u):
        return ref.at[s, u]

    z_copies = []

    def ring(s, u, way):
        to = s + 1 if way == 0 else (s + 7) % 8
        cp = copy(sub(z_own, s, u), sub(z_own, to, u), z_send.at[way, s, u], z_recv.at[to, u], right if way == 0 else left)
        cp.start()
        z_copies.append(cp)

    def share(s, u):
        cp = copy(sub(z_own, s, u), sub(z_oth, s, u), d_send.at[s, u], d_recv.at[s, u], mate)
        cp.start()
        return cp

    shares = []

    def arrived(s, u):
        pltpu.make_async_copy(sub(z_own, s, u), sub(z_own, s, u), z_recv.at[s, u]).wait()

    for u in range(2):
        ring(0, u, 0)
        ring(0, u, 1)
        shares.append(share(0, u))
        if u == 0:
            for cp in z_copies:
                cp.wait_send()
    for s in range(1, 4):
        for u in range(2):
            arrived(s, u)
            if s < 3 or u == 0:
                ring(s, u, 0)
            shares.append(share(s, u))
            arrived(8 - s, u)
            if s < 3 or u == 1:
                ring(8 - s, u, 1)
            shares.append(share(8 - s, u))
    for u in range(2):
        arrived(4, u)
        shares.append(share(4, u))
    for cp in sel_copies:
        cp.wait()
    own_sel.wait()
    pltpu.sync_copy(sel_buf, sel_sm)
    for cp in shares:
        cp.wait()

    def gram(d):
        for i in range(4):
            j = sel_sm[d, lax.rem(i + core, 4), 0]
            choice = sel_buf[d, pl.ds(lax.rem(i + core, 4), 1), :]
            last0 = 2 * x + 1
            last1 = 15 - 2 * x
            below = 2 * (x + 1) + jnp.minimum(j, last1)
            at = slice(128 * i, 128 * i + 128)
            for n, ref in enumerate((z_own, z_oth)):
                part = ref[:, :, j].reshape(128, 128)
                s_high[256 * n : 256 * n + 128, at], s_low[256 * n : 256 * n + 128, at] = split(
                    jnp.where(choice <= last0, part, 0.0)
                )
                part = ref[:, :, below].reshape(128, 128)
                s_high[256 * n + 128 : 256 * n + 256, at], s_low[256 * n + 128 : 256 * n + 256, at] = split(
                    jnp.where(choice <= last1, part, 0.0)
                )

        def cols(a, b):
            return s_high[:, a:b], s_low[:, a:b]

        first = dot(cols(0, 128), cols(0, 384), axis=0)
        second = dot(cols(256, 384), cols(256, 512), axis=0)
        a_send[d, :, 0:128] = first[:, 0:128]
        a_send[d, :, 128:384] = 2.0 * first[:, 128:384]
        a_send[d, :, 384:512] = second[:, 0:128]
        a_send[d, :, 512:640] = 2.0 * second[:, 128:256]

    x_next = device(ylo, lax.rem(x + 1, 4), z, blk)
    x_last = device(ylo, lax.rem(x + 3, 4), z, blk)
    top, bottom = pl.ds(0, 64), pl.ds(64, 64)
    x_copies = [
        copy(a_send.at[2, top], a_pass.at[0], x_send.at[0], x_recv.at[0], x_next),
        copy(a_send.at[2, bottom], a_pass.at[1], x_send.at[1], x_recv.at[1], x_last),
        copy(a_send.at[1, bottom], a_recv.at[0, bottom], x_send.at[2], x_recv.at[2], x_next),
        copy(a_send.at[3, top], a_recv.at[1, top], x_send.at[3], x_recv.at[3], x_last),
        copy(a_send.at[1, top], a_recv.at[0, top], x_send.at[4], x_recv.at[4], x_next),
        copy(a_send.at[3, bottom], a_recv.at[1, bottom], x_send.at[5], x_recv.at[5], x_last),
    ]
    gram(2)
    x_copies[0].start()
    x_copies[1].start()
    gram(1)
    x_copies[2].start()
    gram(3)
    x_copies[3].start()
    gram(0)
    x_copies[0].wait_recv()
    a_send[1, 0:64, :] = a_send[1, 0:64, :] + a_pass[0]
    x_copies[4].start()
    x_copies[1].wait_recv()
    a_send[3, 64:128, :] = a_send[3, 64:128, :] + a_pass[1]
    x_copies[5].start()

    for r in range(4):

        @pl.when(r >= across_blk)
        def _():
            f_copy(1, r).wait_recv()
            f_copy(2, r).start()

    for r in range(2):
        c_copy(1, r).wait_recv()
        c_copy(2, r).start()
    for r in range(4):

        @pl.when(r >= blk)
        def _():
            f_own[r].wait()

        @pl.when(r >= mate_blk)
        def _():
            f_copy(0, r).wait_recv()

        @pl.when(r >= far_blk)
        def _():
            f_copy(2, r).wait_recv()

    square = jnp.zeros((1, 512), jnp.float32)
    for r in range(4):
        rows = slice(256 * r, 256 * r + 256)
        acc = jnp.zeros((256, 512), jnp.float32)
        for s in range(r + 1):
            at = slice(256 * s, 256 * s + 256)
            acc = acc + dot(split(f_buf[s, rows, :]), (j_high[at, :], j_low[at, :]))
        v_high[rows, :], v_low[rows, :] = split(acc)
        square = square + jnp.sum(acc * acc, axis=0, keepdims=True)

    for r in range(2):
        c_own[r].wait()
        c_copy(0, r).wait_recv()
        c_copy(2, r).wait_recv()
    for q in range(4):
        rows = lax.broadcasted_iota(jnp.int32, (128, 512), 0) + q * 128
        root = jnp.zeros((128, 512), jnp.float32)
        for k in range(2):
            root = root + jnp.where(rows == jri_ref[k : k + 1, :], jrv_ref[k : k + 1, :], 0.0)
        acc = -root
        for s in range(4):
            at = slice(256 * s, 256 * s + 256)
            acc = acc + dot(split(c_buf[s, 128 * q : 128 * q + 128, :]), (v_high[at, :], v_low[at, :]))
        at = slice(128 * q, 128 * q + 128)
        g_buf[at, :] = acc
        g_high[at, :], g_low[at, :] = split(acc)
        if q == 0:
            g_buf[512:640, :] = acc
            g_high[512:640, :], g_low[512:640, :] = split(acc)

    for cp in x_copies[2:]:
        cp.wait_recv()
    a_sum[0] = a_send[0] + a_recv[0] + a_recv[1]
    a_share = copy(a_sum.at[0], a_sum.at[1], as_send, as_recv, mate)
    a_share.start()

    def quad(n, c):
        total = jnp.zeros((1, 512), jnp.float32)
        for a, b, off in ((0, 384, 0), (384, 640, 256)):
            start = pl.multiple_of(c * 128 + off, 128)
            at = pl.ds(start, b - a)
            w = dot(split(a_sum[n, :, a:b]), (g_high[at, :], g_low[at, :]))
            total = total + jnp.sum(w * g_buf[pl.ds(start, 128), :], axis=0, keepdims=True)
        return total

    omega = noise_ref[...] + square + quad(0, core)
    a_share.wait()
    omega = omega + quad(1, 1 - core)
    live = lax.broadcasted_iota(jnp.int32, (1, 512), 1) < count_ref[0]
    out_ref[...] = jnp.where(live, resid_ref[...] / jnp.sqrt(omega), 0.0)

    for key in spread:

        @pl.when(spread_valid(*key)[0])
        def _():
            copy(*spread_copy(*key)).wait_send()

    for cp in z_copies[2:]:
        cp.wait_send()
    for cp in x_copies:
        cp.wait_send()
    for r in range(4):

        @pl.when(r >= blk)
        def _():
            f_copy(0, r).wait_send()
            f_copy(1, r).wait_send()

        @pl.when(r >= across_blk)
        def _():
            f_copy(2, r).wait_send()

    for r in range(2):
        for kind in range(3):
            c_copy(kind, r).wait_send()


def per_device(root, front, coupling, blocks, jci, jcv, jri, jrv, resid, noise, count):
    vmem = pl.BlockSpec(memory_space=pltpu.VMEM)
    dma = pltpu.SemaphoreType.DMA
    f32, bf16 = jnp.float32, jnp.bfloat16
    out = pl.pallas_call(
        kernel,
        out_shape=jax.ShapeDtypeStruct((1, 512), f32),
        in_specs=[pl.BlockSpec(memory_space=pltpu.HBM)] * 11,
        out_specs=vmem,
        scratch_shapes=[
            pltpu.VMEM((32, 512), f32),
            pltpu.VMEM((8, 128), jnp.int32),
            pltpu.VMEM((6, 512), jnp.int32),
            pltpu.VMEM((6, 512), f32),
            pltpu.VMEM((2, 512), jnp.int32),
            pltpu.VMEM((2, 512), f32),
            pltpu.VMEM((1, 512), f32),
            pltpu.VMEM((1, 512), f32),
            pltpu.SMEM((1, 4), jnp.int32),
            pltpu.SMEM((1,), jnp.int32),
            dma((9,)),
            pltpu.VMEM((2, 2, 2, 2, 8, 128), f32),
            pltpu.VMEM((8, 2, TILES, 8, 128), f32),
            pltpu.VMEM((8, 2, TILES, 8, 128), f32),
            pltpu.VMEM((4, 1024, 256), f32),
            pltpu.VMEM((4, 512, 256), f32),
            pltpu.VMEM((1024, 512), bf16),
            pltpu.VMEM((1024, 512), bf16),
            pltpu.VMEM((1024, 512), bf16),
            pltpu.VMEM((1024, 512), bf16),
            pltpu.VMEM((640, 512), f32),
            pltpu.VMEM((640, 512), bf16),
            pltpu.VMEM((640, 512), bf16),
            pltpu.VMEM((512, 512), bf16),
            pltpu.VMEM((512, 512), bf16),
            pltpu.VMEM((4, 128, 640), f32),
            pltpu.VMEM((2, 64, 640), f32),
            pltpu.VMEM((2, 128, 640), f32),
            pltpu.VMEM((2, 128, 640), f32),
            pltpu.VMEM((4, 8, 128), jnp.int32),
            pltpu.SMEM((4, 8, 128), jnp.int32),
            dma((2, 2, 4)), dma((9,)), dma((2, 8, 2)), dma((8, 2)), dma((8, 2)), dma((8, 2)),
            dma((4,)), dma((4,)),
            dma((3, 4)), dma((4, 4)), dma((3, 2)), dma((4, 2)),
            dma((6,)), dma((6,)), dma, dma,
        ],
        compiler_params=pltpu.CompilerParams(
            collective_id=0, has_side_effects=True, vmem_limit_bytes=63 << 20
        ),
        name="selected_inverse",
    )(
        root, front, coupling, blocks, jci, jcv, jri, jrv,
        resid.reshape(1, -1), noise.reshape(1, -1), count,
    )
    return out.reshape(-1)


def solution(mesh):
    placed = (
        P("leaf", "blk"),
        P("leaf", "blk"),
        P("leaf", "blk"),
        P("leaf", None),
        P(None, ("leaf", "blk")),
        P(None, ("leaf", "blk")),
        P(None, ("leaf", "blk")),
        P(None, ("leaf", "blk")),
        P(("leaf", "blk")),
        P(("leaf", "blk")),
        P(("leaf", "blk")),
    )
    return jax.shard_map(
        per_device, mesh=mesh, in_specs=placed, out_specs=P(("leaf", "blk")), check_vma=False
    )
```

time: 64.4 us -> 58 us (0.901)
  local copies, waits for them, and re-layouts: 5.74 us -> 1.26 us
  Pallas kernels: 57.2 us -> 56 us
    unnamed x21 -> x1, local copies, waits for them, and re-layouts: 5.67 us -> 1.26 us
    pallas_call x1, Pallas kernels: 57.2 us -> 56 us  [per_device(): pl.pallas_call(kernel, out_shape=jax.ShapeDtypeStruct((1, 512), f32), in_...]
where the time goes in v2:
time: 58 us; the launch traced here: 57.9 us
  Pallas kernels  56 us (97%)
  local copies, waits for them, and re-layouts  1.26 us (2%)
  between operations  0.66 us (1%)
    pallas_call x1, Pallas kernels, per_device(): pl.pallas_call(kernel, out_shape=jax.ShapeDtypeStruct((1, 512), f32), in_...  56 us
    unnamed x1, local copies, waits for them, and re-layouts  1.26 us

profile of v2, /device:TPU:25, one launch (start us, length us, event | category | flops | bytes accessed | tf_op | source)
XLA Modules:
  0.0 57.9 jit_solution(10715708382679272001)
XLA Ops:
  0.7 56.0 %selected_inverse.1 = f32[1,512]{1,0:T(1,128)} custom-call(f32[32,512]{1,0:T(8,128)} %l_hbm.1, f32[1024,256]{1,0:T(8,128)} %f_ref.1, f32[512,256]{1,0:T(8,128)} %c_ref.1, s32[1,4]{1,0:T(1,128)} %sel_hbm.1, s32[6,512]{1,0:T(8,128)} %jci_hbm.1, f32[6,512]{1,0:T(8,128)} %jcv_hbm.1, s32[2,512]{1,0:T(2,128)} %jri_hbm.1, f32[2,512]{1,0:T(2,128)} %jrv_hbm.1, ...), custom_call_target="tpu_custom_call" | custom-call | tf_op jit(solution)/shard_map/selected_inverse/pallas_call | solution.py:400
  56.6 1.3 %copy.14 = f32[512]{0:T(512)} copy(f32[512]{0:T(512)} %bitcast.3) | data formatting | bytes 4096

commit v3 on v2

--- a/solution.py
+++ b/solution.py
@@ -64,6 +64,8 @@
     ]
     for cp in loads:
         cp.start()
+
+    a_send[:, 128:136, :] = jnp.zeros((4, 8, 512), jnp.float32)
 
     barrier = pltpu.get_barrier_semaphore()
     mirror = 3 - x
@@ -191,7 +193,7 @@
         pltpu.make_async_copy(tile, tile, l_recv.at[slot]).wait()
 
     def sub(ref, s, u):
-        return ref.at[s, u]
+        return ref.at[s, u // 2, pl.ds(9 * (u % 2), 9)]
 
     z_copies = []
 
@@ -211,24 +213,23 @@
     def arrived(s, u):
         pltpu.make_async_copy(sub(z_own, s, u), sub(z_own, s, u), z_recv.at[s, u]).wait()
 
-    for u in range(2):
+    for u in range(4):
         ring(0, u, 0)
-        ring(0, u, 1)
+        ring(0, 3 - u, 1)
+    for u in range(4):
         shares.append(share(0, u))
-        if u == 0:
-            for cp in z_copies:
-                cp.wait_send()
     for s in range(1, 4):
-        for u in range(2):
+        for u in range(4):
             arrived(s, u)
-            if s < 3 or u == 0:
+            if s < 3 or u < 2:
                 ring(s, u, 0)
             shares.append(share(s, u))
-            arrived(8 - s, u)
-            if s < 3 or u == 1:
-                ring(8 - s, u, 1)
-            shares.append(share(8 - s, u))
-    for u in range(2):
+            w = 3 - u
+            arrived(8 - s, w)
+            if s < 3 or w >= 2:
+                ring(8 - s, w, 1)
+            shares.append(share(8 - s, w))
+    for u in (0, 3, 1, 2):
         arrived(4, u)
         shares.append(share(4, u))
     for cp in sel_copies:
@@ -237,6 +238,9 @@
     pltpu.sync_copy(sel_buf, sel_sm)
     for cp in shares:
         cp.wait()
+
+    row_is = lax.broadcasted_iota(jnp.int32, (128, 128), 0)
+    col_is = lax.broadcasted_iota(jnp.int32, (128, 128), 1)
 
     def gram(d):
         for i in range(4):
@@ -261,17 +265,21 @@
 
         first = dot(cols(0, 128), cols(0, 384), axis=0)
         second = dot(cols(256, 384), cols(256, 512), axis=0)
-        a_send[d, :, 0:128] = first[:, 0:128]
-        a_send[d, :, 128:384] = 2.0 * first[:, 128:384]
-        a_send[d, :, 384:512] = second[:, 0:128]
-        a_send[d, :, 512:640] = 2.0 * second[:, 128:256]
+        a_send[d, 0:128, 0:128] = jnp.where(
+            row_is > col_is, 2.0 * first[:, 0:128], jnp.where(row_is == col_is, first[:, 0:128], 2.0 * second[:, 0:128])
+        )
+        a_send[d, 128:136, 0:128] = jnp.broadcast_to(
+            jnp.sum(jnp.where(row_is == col_is, second[:, 0:128], 0.0), axis=0, keepdims=True), (8, 128)
+        )
+        a_send[d, 0:128, 128:384] = 2.0 * first[:, 128:384]
+        a_send[d, 0:128, 384:512] = 2.0 * second[:, 128:256]
 
     x_next = device(ylo, lax.rem(x + 1, 4), z, blk)
     x_last = device(ylo, lax.rem(x + 3, 4), z, blk)
-    top, bottom = pl.ds(0, 64), pl.ds(64, 64)
+    top, bottom = pl.ds(0, 64), pl.ds(64, 72)
     x_copies = [
-        copy(a_send.at[2, top], a_pass.at[0], x_send.at[0], x_recv.at[0], x_next),
-        copy(a_send.at[2, bottom], a_pass.at[1], x_send.at[1], x_recv.at[1], x_last),
+        copy(a_send.at[2, top], a_pass.at[pl.ds(0, 64)], x_send.at[0], x_recv.at[0], x_next),
+        copy(a_send.at[2, bottom], a_pass.at[pl.ds(64, 72)], x_send.at[1], x_recv.at[1], x_last),
         copy(a_send.at[1, bottom], a_recv.at[0, bottom], x_send.at[2], x_recv.at[2], x_next),
         copy(a_send.at[3, top], a_recv.at[1, top], x_send.at[3], x_recv.at[3], x_last),
         copy(a_send.at[1, top], a_recv.at[0, top], x_send.at[4], x_recv.at[4], x_next),
@@ -286,10 +294,10 @@
     x_copies[3].start()
     gram(0)
     x_copies[0].wait_recv()
-    a_send[1, 0:64, :] = a_send[1, 0:64, :] + a_pass[0]
+    a_send[1, 0:64, :] = a_send[1, 0:64, :] + a_pass[0:64, :]
     x_copies[4].start()
     x_copies[1].wait_recv()
-    a_send[3, 64:128, :] = a_send[3, 64:128, :] + a_pass[1]
+    a_send[3, 64:136, :] = a_send[3, 64:136, :] + a_pass[64:136, :]
     x_copies[5].start()
 
     for r in range(4):
@@ -353,12 +361,18 @@
     a_share.start()
 
     def quad(n, c):
+        both = a_sum[n, 0:128, 0:128]
+        lower = jnp.where(row_is >= col_is, both, 0.0)
+        diagonal = jnp.where(row_is == col_is, a_sum[n, 128:129, 0:128], 0.0)
+        upper_ = jnp.where(row_is < col_is, both, diagonal)
         total = jnp.zeros((1, 512), jnp.float32)
-        for a, b, off in ((0, 384, 0), (384, 640, 256)):
+        for corner, a, b, off in ((lower, 128, 384, 0), (upper_, 384, 512, 256)):
             start = pl.multiple_of(c * 128 + off, 128)
-            at = pl.ds(start, b - a)
-            w = dot(split(a_sum[n, :, a:b]), (g_high[at, :], g_low[at, :]))
-            total = total + jnp.sum(w * g_buf[pl.ds(start, 128), :], axis=0, keepdims=True)
+            near_ = pl.ds(start, 128)
+            after = pl.ds(pl.multiple_of(start + 128, 128), b - a)
+            w = dot(split(corner), (g_high[near_, :], g_low[near_, :]))
+            w = w + dot(split(a_sum[n, 0:128, a:b]), (g_high[after, :], g_low[after, :]))
+            total = total + jnp.sum(w * g_buf[near_, :], axis=0, keepdims=True)
         return total
 
     omega = noise_ref[...] + square + quad(0, core)
@@ -373,7 +387,7 @@
         def _():
             copy(*spread_copy(*key)).wait_send()
 
-    for cp in z_copies[2:]:
+    for cp in z_copies:
         cp.wait_send()
     for cp in x_copies:
         cp.wait_send()
@@ -428,13 +442,13 @@
             pltpu.VMEM((640, 512), bf16),
             pltpu.VMEM((512, 512), bf16),
             pltpu.VMEM((512, 512), bf16),
-            pltpu.VMEM((4, 128, 640), f32),
-            pltpu.VMEM((2, 64, 640), f32),
-            pltpu.VMEM((2, 128, 640), f32),
-            pltpu.VMEM((2, 128, 640), f32),
+            pltpu.VMEM((4, 136, 512), f32),
+            pltpu.VMEM((136, 512), f32),
+            pltpu.VMEM((2, 136, 512), f32),
+            pltpu.VMEM((2, 136, 512), f32),
             pltpu.VMEM((4, 8, 128), jnp.int32),
             pltpu.SMEM((4, 8, 128), jnp.int32),
-            dma((2, 2, 4)), dma((9,)), dma((2, 8, 2)), dma((8, 2)), dma((8, 2)), dma((8, 2)),
+            dma((2, 2, 4)), dma((9,)), dma((2, 8, 4)), dma((8, 4)), dma((8, 4)), dma((8, 4)),
             dma((4,)), dma((4,)),
             dma((3, 4)), dma((4, 4)), dma((3, 2)), dma((4, 2)),
             dma((6,)), dma((6,)), dma, dma,

time: 58 us -> 55.2 us (0.952)
  Pallas kernels: 56 us -> 53.1 us
    pallas_call x1, Pallas kernels: 56 us -> 53.1 us  [per_device(): pl.pallas_call(kernel, out_shape=jax.ShapeDtypeStruct((1, 512), f32), in_...]
where the time goes in v3:
time: 55.2 us; the launch traced here: 55 us
  Pallas kernels  53.1 us (96%)
  local copies, waits for them, and re-layouts  1.26 us (2%)
  between operations  0.66 us (1%)
    pallas_call x1, Pallas kernels, per_device(): pl.pallas_call(kernel, out_shape=jax.ShapeDtypeStruct((1, 512), f32), in_...  53.1 us
    unnamed x1, local copies, waits for them, and re-layouts  1.26 us

profile of v3, /device:TPU:25, one launch (start us, length us, event | category | flops | bytes accessed | tf_op | source)
XLA Modules:
  0.0 55.0 jit_solution(745884131502827348)
XLA Ops:
  0.7 53.1 %selected_inverse.1 = f32[1,512]{1,0:T(1,128)} custom-call(f32[32,512]{1,0:T(8,128)} %l_hbm.1, f32[1024,256]{1,0:T(8,128)} %f_ref.1, f32[512,256]{1,0:T(8,128)} %c_ref.1, s32[1,4]{1,0:T(1,128)} %sel_hbm.1, s32[6,512]{1,0:T(8,128)} %jci_hbm.1, f32[6,512]{1,0:T(8,128)} %jcv_hbm.1, s32[2,512]{1,0:T(2,128)} %jri_hbm.1, f32[2,512]{1,0:T(2,128)} %jrv_hbm.1, ...), custom_call_target="tpu_custom_call" | custom-call | tf_op jit(solution)/shard_map/selected_inverse/pallas_call | solution.py:414
  53.7 1.3 %copy.14 = f32[512]{0:T(512)} copy(f32[512]{0:T(512)} %bitcast.3) | data formatting | bytes 4096

commit v4 on v3

--- a/solution.py
+++ b/solution.py
@@ -8,6 +8,8 @@
 from jax.sharding import PartitionSpec as P
 
 MESH = pl.DeviceIdType.MESH
+CROSS_AT = 2
+PIECES = 4
 TILES = 18
 
 
@@ -62,9 +64,7 @@
             ]
         )
     ]
-    for cp in loads:
-        cp.start()
-
+    loads[0].start()
     a_send[:, 128:136, :] = jnp.zeros((4, 8, 512), jnp.float32)
 
     barrier = pltpu.get_barrier_semaphore()
@@ -80,49 +80,54 @@
                 partners.append(device(lax.rem(ylo + d_ylo, 2), x, z, lax.rem(blk + d_blk, 4)))
     for p in partners:
         pl.semaphore_signal(barrier, inc=1, device_id=p, device_id_type=MESH)
+    for cp in loads[1:]:
+        cp.start()
     loads[0].wait()
+    for h in range(2):
+        for core_d in range(2):
+            for u in range(2):
+                for q in range(2):
+                    r, c = 16 * core_d + 8 * u, 256 * h + 128 * q
+                    l_buf[core_d, u, 2 * h + q] = l_ref[r : r + 8, c : c + 128]
+    pl.semaphore_wait(barrier, len(partners))
+
+    upper = ylo == 0
+    spread = [(ylo_d, blk_d) for ylo_d in range(2) for blk_d in range(4)]
+    x_to = jnp.where(upper, x, mirror)
+    slot_to = jnp.where(upper, 0, 4 - x) + 2 * blk
+    tiles_out = jnp.clip(jnp.where(upper, x, 4 + x) + 1 - 2 * blk, 0, 2)
+
+    def spread_copy(n, ylo_d, blk_d):
+        return (
+            l_buf.at[blk_d % 2, :, pl.ds(0, 2 * n)], z_own.at[0, :, pl.ds(2 * slot_to, 2 * n)],
+            l_send.at[ylo_d, blk_d], l_recv.at[jnp.where(upper, blk, 2 + blk)], device(ylo_d, x_to, z, blk_d),
+        )
+
+    def spread_mine(ylo_d, blk_d):
+        return upper & (ylo_d == ylo) & (blk_d == blk)
+
+    for n in (1, 2):
+
+        @pl.when(tiles_out == n)
+        def _():
+            for key in spread:
+                mine = spread_mine(*key)
+
+                @pl.when(jnp.logical_not(mine))
+                def _():
+                    copy(*spread_copy(n, *key)).start()
+
+                @pl.when(mine)
+                def _():
+                    src, dst, _, sem, _ = spread_copy(n, *key)
+                    pltpu.make_async_copy(src, dst, sem).start()
+
     loads[1].wait()
     row = lax.broadcasted_iota(jnp.int32, (8, 128), 0)
     choices = jnp.zeros((8, 128), jnp.int32)
     for i in range(4):
         choices = jnp.where(row == i, sel_own[0, i], choices)
     sel_ref[...] = choices
-    for h in range(2):
-        for core_d in range(2):
-            for u in range(2):
-                for q in range(2):
-                    r, c = 16 * core_d + 8 * u, 256 * h + 128 * q
-                    l_buf[h, core_d, u, q] = l_ref[r : r + 8, c : c + 128]
-    pl.semaphore_wait(barrier, len(partners))
-
-    upper = ylo == 0
-    spread = [(h, ylo_d, blk_d) for h in range(2) for ylo_d in range(2) for blk_d in range(4)]
-    x_to = jnp.where(upper, x, mirror)
-
-    def spread_copy(h, ylo_d, blk_d):
-        slot = jnp.where(upper, 0, 4 - x) + 2 * blk + h
-        return (
-            l_buf.at[h, blk_d % 2], z_own.at[0, :, pl.ds(2 * slot, 2)],
-            l_send.at[h, ylo_d, blk_d], l_recv.at[slot], device(ylo_d, x_to, z, blk_d),
-        )
-
-    def spread_valid(h, ylo_d, blk_d):
-        valid = 2 * blk + h <= jnp.where(upper, x, 4 + x)
-        mine = upper & (ylo_d == ylo) & (blk_d == blk)
-        return valid & jnp.logical_not(mine), valid & mine
-
-    for key in spread:
-        away, here = spread_valid(*key)
-
-        @pl.when(away)
-        def _():
-            copy(*spread_copy(*key)).start()
-
-        @pl.when(here)
-        def _():
-            src, dst, _, sem, _ = spread_copy(*key)
-            pltpu.make_async_copy(src, dst, sem).start()
-
     sel_copies = []
     for d in range(1, 4):
         cp = copy(
@@ -165,8 +170,6 @@
             def _():
                 f_copy(kind, r).start()
 
-        for r in range(2):
-            c_copy(kind, r).start()
     for r in range(4):
 
         @pl.when(r >= blk)
@@ -174,6 +177,7 @@
             f_own[r].start()
 
     for r in range(2):
+        c_copy(0, r).start()
         c_own[r].start()
 
     for cp in loads[2:]:
@@ -188,12 +192,19 @@
         at = pl.ds(pl.multiple_of(i * 64, 64), 64)
         j_high[at, :], j_low[at, :] = split(acc)
 
-    for slot in range(9):
-        tile = z_own.at[0, :, pl.ds(2 * slot, 2)]
-        pltpu.make_async_copy(tile, tile, l_recv.at[slot]).wait()
+    for source in range(6):
+        half, b = source // 2 > 0, source if source < 2 else source - 2
+        tiles_in = jnp.clip((7 - x if half else x) + 1 - 2 * b, 0, 2)
+        first = (x + 1 if half else 0) + 2 * b
+        for n in (1, 2):
+
+            @pl.when(tiles_in == n)
+            def _():
+                area = z_own.at[0, :, pl.ds(2 * first, 2 * n)]
+                pltpu.make_async_copy(area, area, l_recv.at[source]).wait()
 
     def sub(ref, s, u):
-        return ref.at[s, u // 2, pl.ds(9 * (u % 2), 9)]
+        return ref.at[s, u // (PIECES // 2), pl.ds(u % (PIECES // 2) * (2 * TILES // PIECES), 2 * TILES // PIECES)]
 
     z_copies = []
 
@@ -203,8 +214,8 @@
         cp.start()
         z_copies.append(cp)
 
-    def share(s, u):
-        cp = copy(sub(z_own, s, u), sub(z_oth, s, u), d_send.at[s, u], d_recv.at[s, u], mate)
+    def share(s):
+        cp = copy(z_own.at[s], z_oth.at[s], d_send.at[s], d_recv.at[s], mate)
         cp.start()
         return cp
 
@@ -213,25 +224,28 @@
     def arrived(s, u):
         pltpu.make_async_copy(sub(z_own, s, u), sub(z_own, s, u), z_recv.at[s, u]).wait()
 
-    for u in range(4):
+    for u in range(PIECES):
         ring(0, u, 0)
-        ring(0, 3 - u, 1)
-    for u in range(4):
-        shares.append(share(0, u))
+        ring(0, PIECES - 1 - u, 1)
+    shares.append(share(0))
     for s in range(1, 4):
-        for u in range(4):
+        if s == CROSS_AT:
+            for r in range(2):
+                c_copy(1, r).start()
+        for u in range(PIECES):
             arrived(s, u)
-            if s < 3 or u < 2:
+            if s < 3 or u < PIECES // 2:
                 ring(s, u, 0)
-            shares.append(share(s, u))
-            w = 3 - u
+            w = PIECES - 1 - u
             arrived(8 - s, w)
-            if s < 3 or w >= 2:
+            if s < 3 or w >= PIECES // 2:
                 ring(8 - s, w, 1)
-            shares.append(share(8 - s, w))
-    for u in (0, 3, 1, 2):
-        arrived(4, u)
-        shares.append(share(4, u))
+        shares.append(share(s))
+        shares.append(share(8 - s))
+    for v in range(PIECES // 2):
+        for u in (v, PIECES - 1 - v):
+            arrived(4, u)
+    shares.append(share(4))
     for cp in sel_copies:
         cp.wait()
     own_sel.wait()
@@ -288,6 +302,13 @@
     gram(2)
     x_copies[0].start()
     x_copies[1].start()
+    for r in range(4):
+
+        @pl.when(r >= across_blk)
+        def _():
+            f_copy(1, r).wait_recv()
+            f_copy(2, r).start()
+
     gram(1)
     x_copies[2].start()
     gram(3)
@@ -299,13 +320,6 @@
     x_copies[1].wait_recv()
     a_send[3, 64:136, :] = a_send[3, 64:136, :] + a_pass[64:136, :]
     x_copies[5].start()
-
-    for r in range(4):
-
-        @pl.when(r >= across_blk)
-        def _():
-            f_copy(1, r).wait_recv()
-            f_copy(2, r).start()
 
     for r in range(2):
         c_copy(1, r).wait_recv()
@@ -381,11 +395,15 @@
     live = lax.broadcasted_iota(jnp.int32, (1, 512), 1) < count_ref[0]
     out_ref[...] = jnp.where(live, resid_ref[...] / jnp.sqrt(omega), 0.0)
 
-    for key in spread:
-
-        @pl.when(spread_valid(*key)[0])
-        def _():
-            copy(*spread_copy(*key)).wait_send()
+    for n in (1, 2):
+
+        @pl.when(tiles_out == n)
+        def _():
+            for key in spread:
+
+                @pl.when(jnp.logical_not(spread_mine(*key)))
+                def _():
+                    copy(*spread_copy(n, *key)).wait_send()
 
     for cp in z_copies:
         cp.wait_send()
@@ -428,7 +446,7 @@
             pltpu.SMEM((1, 4), jnp.int32),
             pltpu.SMEM((1,), jnp.int32),
             dma((9,)),
-            pltpu.VMEM((2, 2, 2, 2, 8, 128), f32),
+            pltpu.VMEM((2, 2, 4, 8, 128), f32),
             pltpu.VMEM((8, 2, TILES, 8, 128), f32),
             pltpu.VMEM((8, 2, TILES, 8, 128), f32),
             pltpu.VMEM((4, 1024, 256), f32),
@@ -448,7 +466,7 @@
             pltpu.VMEM((2, 136, 512), f32),
             pltpu.VMEM((4, 8, 128), jnp.int32),
             pltpu.SMEM((4, 8, 128), jnp.int32),
-            dma((2, 2, 4)), dma((9,)), dma((2, 8, 4)), dma((8, 4)), dma((8, 4)), dma((8, 4)),
+            dma((2, 4)), dma((6,)), dma((2, 8, PIECES)), dma((8, PIECES)), dma((8,)), dma((8,)),
             dma((4,)), dma((4,)),
             dma((3, 4)), dma((4, 4)), dma((3, 2)), dma((4, 2)),
             dma((6,)), dma((6,)), dma, dma,

time: 55.2 us -> 53.9 us (0.976)
  Pallas kernels: 53.1 us -> 51.8 us
    pallas_call x1, Pallas kernels: 53.1 us -> 51.8 us  [per_device(): pl.pallas_call(kernel, out_shape=jax.ShapeDtypeStruct((1, 512), f32), in_...]
where the time goes in v4:
time: 53.9 us; the launch traced here: 53.7 us
  Pallas kernels  51.8 us (96%)
  local copies, waits for them, and re-layouts  1.26 us (2%)
  between operations  0.66 us (1%)
    pallas_call x1, Pallas kernels, per_device(): pl.pallas_call(kernel, out_shape=jax.ShapeDtypeStruct((1, 512), f32), in_...  51.8 us
    unnamed x1, local copies, waits for them, and re-layouts  1.26 us

profile of v4, /device:TPU:25, one launch (start us, length us, event | category | flops | bytes accessed | tf_op | source)
XLA Modules:
  0.0 53.7 jit_solution(1833338819815156055)
XLA Ops:
  0.7 51.8 %selected_inverse.1 = f32[1,512]{1,0:T(1,128)} custom-call(f32[32,512]{1,0:T(8,128)} %l_hbm.1, f32[1024,256]{1,0:T(8,128)} %f_ref.1, f32[512,256]{1,0:T(8,128)} %c_ref.1, s32[1,4]{1,0:T(1,128)} %sel_hbm.1, s32[6,512]{1,0:T(8,128)} %jci_hbm.1, f32[6,512]{1,0:T(8,128)} %jcv_hbm.1, s32[2,512]{1,0:T(2,128)} %jri_hbm.1, f32[2,512]{1,0:T(2,128)} %jrv_hbm.1, ...), custom_call_target="tpu_custom_call" | custom-call | tf_op jit(solution)/shard_map/selected_inverse/pallas_call | solution.py:432
  52.4 1.3 %copy.14 = f32[512]{0:T(512)} copy(f32[512]{0:T(512)} %bitcast.3) | data formatting | bytes 4096

commit v5 on v4

--- a/solution.py
+++ b/solution.py
@@ -321,9 +321,6 @@
     a_send[3, 64:136, :] = a_send[3, 64:136, :] + a_pass[64:136, :]
     x_copies[5].start()
 
-    for r in range(2):
-        c_copy(1, r).wait_recv()
-        c_copy(2, r).start()
     for r in range(4):
 
         @pl.when(r >= blk)
@@ -347,12 +344,16 @@
             acc = acc + dot(split(f_buf[s, rows, :]), (j_high[at, :], j_low[at, :]))
         v_high[rows, :], v_low[rows, :] = split(acc)
         square = square + jnp.sum(acc * acc, axis=0, keepdims=True)
-
-    for r in range(2):
-        c_own[r].wait()
-        c_copy(0, r).wait_recv()
-        c_copy(2, r).wait_recv()
+        if r == 2:
+            for r in range(2):
+                c_copy(1, r).wait_recv()
+                c_copy(2, r).start()
+
     for q in range(4):
+        if q % 2 == 0:
+            c_own[q // 2].wait()
+            c_copy(0, q // 2).wait_recv()
+            c_copy(2, q // 2).wait_recv()
         rows = lax.broadcasted_iota(jnp.int32, (128, 512), 0) + q * 128
         root = jnp.zeros((128, 512), jnp.float32)
         for k in range(2):

time: 53.9 us -> 53.5 us (level)
  no operation moved by 1% of the time
where the time goes in v5:
time: 53.5 us; the launch traced here: 53.3 us
  Pallas kernels  51.4 us (96%)
  local copies, waits for them, and re-layouts  1.26 us (2%)
  between operations  0.66 us (1%)
    pallas_call x1, Pallas kernels, per_device(): pl.pallas_call(kernel, out_shape=jax.ShapeDtypeStruct((1, 512), f32), in_...  51.4 us
    unnamed x1, local copies, waits for them, and re-layouts  1.26 us

profile of v5, /device:TPU:25, one launch (start us, length us, event | category | flops | bytes accessed | tf_op | source)
XLA Modules:
  0.0 53.3 jit_solution(11584078966461061031)
XLA Ops:
  0.7 51.4 %selected_inverse.1 = f32[1,512]{1,0:T(1,128)} custom-call(f32[32,512]{1,0:T(8,128)} %l_hbm.1, f32[1024,256]{1,0:T(8,128)} %f_ref.1, f32[512,256]{1,0:T(8,128)} %c_ref.1, s32[1,4]{1,0:T(1,128)} %sel_hbm.1, s32[6,512]{1,0:T(8,128)} %jci_hbm.1, f32[6,512]{1,0:T(8,128)} %jcv_hbm.1, s32[2,512]{1,0:T(2,128)} %jri_hbm.1, f32[2,512]{1,0:T(2,128)} %jrv_hbm.1, ...), custom_call_target="tpu_custom_call" | custom-call | tf_op jit(solution)/shard_map/selected_inverse/pallas_call | solution.py:433
  52.1 1.3 %copy.14 = f32[512]{0:T(512)} copy(f32[512]{0:T(512)} %bitcast.3) | data formatting | bytes 4096

commit v6 on v5

--- a/solution.py
+++ b/solution.py
@@ -92,7 +92,7 @@
     pl.semaphore_wait(barrier, len(partners))
 
     upper = ylo == 0
-    spread = [(ylo_d, blk_d) for ylo_d in range(2) for blk_d in range(4)]
+    spread = [(ylo_d, blk_d) for blk_d in range(4) for ylo_d in range(2)]
     x_to = jnp.where(upper, x, mirror)
     slot_to = jnp.where(upper, 0, 4 - x) + 2 * blk
     tiles_out = jnp.clip(jnp.where(upper, x, 4 + x) + 1 - 2 * blk, 0, 2)

time: 53.5 us -> 53.3 us (level)
  no operation moved by 1% of the time
where the time goes in v6:
time: 53.3 us; the launch traced here: 53.1 us
  Pallas kernels  51.2 us (96%)
  local copies, waits for them, and re-layouts  1.26 us (2%)
  between operations  0.66 us (1%)
    pallas_call x1, Pallas kernels, per_device(): pl.pallas_call(kernel, out_shape=jax.ShapeDtypeStruct((1, 512), f32), in_...  51.2 us
    unnamed x1, local copies, waits for them, and re-layouts  1.26 us

profile of v6, /device:TPU:25, one launch (start us, length us, event | category | flops | bytes accessed | tf_op | source)
XLA Modules:
  0.0 53.1 jit_solution(15735892995441434384)
XLA Ops:
  0.7 51.2 %selected_inverse.1 = f32[1,512]{1,0:T(1,128)} custom-call(f32[32,512]{1,0:T(8,128)} %l_hbm.1, f32[1024,256]{1,0:T(8,128)} %f_ref.1, f32[512,256]{1,0:T(8,128)} %c_ref.1, s32[1,4]{1,0:T(1,128)} %sel_hbm.1, s32[6,512]{1,0:T(8,128)} %jci_hbm.1, f32[6,512]{1,0:T(8,128)} %jcv_hbm.1, s32[2,512]{1,0:T(2,128)} %jri_hbm.1, f32[2,512]{1,0:T(2,128)} %jrv_hbm.1, ...), custom_call_target="tpu_custom_call" | custom-call | tf_op jit(solution)/shard_map/selected_inverse/pallas_call | solution.py:433
  51.9 1.3 %copy.14 = f32[512]{0:T(512)} copy(f32[512]{0:T(512)} %bitcast.3) | data formatting | bytes 4096

commit v7 on v6

--- a/solution.py
+++ b/solution.py
@@ -302,6 +302,8 @@
     gram(2)
     x_copies[0].start()
     x_copies[1].start()
+    gram(1)
+    x_copies[2].start()
     for r in range(4):
 
         @pl.when(r >= across_blk)
@@ -309,8 +311,6 @@
             f_copy(1, r).wait_recv()
             f_copy(2, r).start()
 
-    gram(1)
-    x_copies[2].start()
     gram(3)
     x_copies[3].start()
     gram(0)

time: 53.3 us -> 53.3 us (level)
  no operation moved by 1% of the time
where the time goes in v7:
time: 53.3 us; the launch traced here: 53.1 us
  Pallas kernels  51.2 us (96%)
  local copies, waits for them, and re-layouts  1.26 us (2%)
  between operations  0.66 us (1%)
    pallas_call x1, Pallas kernels, per_device(): pl.pallas_call(kernel, out_shape=jax.ShapeDtypeStruct((1, 512), f32), in_...  51.2 us
    unnamed x1, local copies, waits for them, and re-layouts  1.26 us

profile of v7, /device:TPU:25, one launch (start us, length us, event | category | flops | bytes accessed | tf_op | source)
XLA Modules:
  0.0 53.1 jit_solution(8100954957728745335)
XLA Ops:
  0.7 51.2 %selected_inverse.1 = f32[1,512]{1,0:T(1,128)} custom-call(f32[32,512]{1,0:T(8,128)} %l_hbm.1, f32[1024,256]{1,0:T(8,128)} %f_ref.1, f32[512,256]{1,0:T(8,128)} %c_ref.1, s32[1,4]{1,0:T(1,128)} %sel_hbm.1, s32[6,512]{1,0:T(8,128)} %jci_hbm.1, f32[6,512]{1,0:T(8,128)} %jcv_hbm.1, s32[2,512]{1,0:T(2,128)} %jri_hbm.1, f32[2,512]{1,0:T(2,128)} %jrv_hbm.1, ...), custom_call_target="tpu_custom_call" | custom-call | tf_op jit(solution)/shard_map/selected_inverse/pallas_call | solution.py:433
  51.9 1.3 %copy.14 = f32[512]{0:T(512)} copy(f32[512]{0:T(512)} %bitcast.3) | data formatting | bytes 4096
